TPU v7x, 256 devices: a whole 4x4x8 slice. The times are simulated.
256 devices in a mesh: tok: 4 (over y), row: 8 (over z_hi, core), col: 8 (over z_lo, x).
Axes of the slice: x: 4, y: 4, z: 8 (z_hi: 4, z_lo: 2; z = z_hi * 2 + z_lo), core: 2. Of those that a mesh axis runs over, the one named last changes fastest.
Arguments:
- tokens: bfloat16 [1024, 8192], P('tok', ('row', 'col')), may hold values from -6 to 6
- gate_weight: bfloat16 [8192, 14336], P('row', ('col', 'tok')), may hold values from -0.0625 to 0.0625
- up_weight: bfloat16 [8192, 14336], P('row', ('col', 'tok')), may hold values from -0.0625 to 0.0625
- down_weight: bfloat16 [14336, 8192], P(('col', 'tok'), 'row'), may hold values from -0.046875 to 0.046875
- cotangent: bfloat16 [1024, 8192], P('tok', ('row', 'col')), may hold values from -6 to 6
Outputs:
- block_out: bfloat16 [1024, 8192], P('tok', ('row', 'col'))
- input_grad: bfloat16 [1024, 8192], P('tok', ('row', 'col'))
- gate_grad: bfloat16 [8192, 14336], P('row', ('col', 'tok'))
- up_grad: bfloat16 [8192, 14336], P('row', ('col', 'tok'))
- down_grad: bfloat16 [14336, 8192], P(('col', 'tok'), 'row')
All inputs are finite; a program needn't handle non-finite values.
Results may differ from a plain program's by a relative error of at most 0.0049.
Values may be sent and summed in bfloat16 or wider, within the bound.
A program may use at most 128 MiB of HBM per device.

v0:
```python
import jax
import jax.numpy as jnp
from jax import lax
from jax.sharding import PartitionSpec as P


def activate(gate_sum, up_sum):
    squash = jax.nn.sigmoid(gate_sum)
    swish = gate_sum * squash
    return (swish * up_sum).astype(jnp.bfloat16)


def derive(slope, gate_sum, up_sum):
    squash = jax.nn.sigmoid(gate_sum)
    swish = gate_sum * squash
    gate_slope = (slope * up_sum * squash * (1.0 + gate_sum * (1.0 - squash))).astype(jnp.bfloat16)
    up_slope = (slope * swish).astype(jnp.bfloat16)
    return (gate_slope, up_slope)


def contract_last(left_op, right_op):
    return lax.dot_general(
        left_op, right_op, (((1,), (1,)), ((), ())), preferred_element_type=jnp.float32
    )


def contract_first(left_op, right_op):
    return lax.dot_general(
        left_op, right_op, (((0,), (0,)), ((), ())), preferred_element_type=jnp.float32
    )


def local(tokens, gate_weight, up_weight, down_weight, cotangent):
    features = lax.all_gather(tokens, "col", axis=1, tiled=True)
    gate_tile, up_tile = (
        lax.all_gather(gate_weight, "tok", axis=1, tiled=True),
        lax.all_gather(up_weight, "tok", axis=1, tiled=True),
    )
    down_tile = lax.all_gather(down_weight, "tok", axis=0, tiled=True)
    gate_part = jnp.dot(features, gate_tile, preferred_element_type=jnp.float32)
    up_part = jnp.dot(features, up_tile, preferred_element_type=jnp.float32)
    gate_sum, up_sum = lax.psum((gate_part, up_part), "row")
    hidden = activate(gate_sum, up_sum)
    out_part = jnp.dot(hidden, down_tile, preferred_element_type=jnp.float32)
    block_out = lax.psum_scatter(out_part, "col", scatter_dimension=1, tiled=True).astype(
        jnp.bfloat16
    )
    cot_tile = lax.all_gather(cotangent, "col", axis=1, tiled=True)
    slope_part = contract_last(cot_tile, down_tile)
    slope = lax.psum(slope_part, "row")
    gate_slope, up_slope = derive(slope, gate_sum, up_sum)
    input_part = contract_last(gate_slope, gate_tile) + contract_last(up_slope, up_tile)
    input_grad = lax.psum_scatter(input_part, "col", scatter_dimension=1, tiled=True).astype(
        jnp.bfloat16
    )
    gate_total, up_total = (
        lax.psum_scatter(
            contract_first(features, gate_slope), "tok", scatter_dimension=1, tiled=True
        ),
        lax.psum_scatter(
            contract_first(features, up_slope), "tok", scatter_dimension=1, tiled=True
        ),
    )
    down_total = lax.psum_scatter(
        contract_first(hidden, cot_tile), "tok", scatter_dimension=0, tiled=True
    )
    return (
        block_out,
        input_grad,
        gate_total.astype(jnp.bfloat16),
        up_total.astype(jnp.bfloat16),
        down_total.astype(jnp.bfloat16),
    )


def solution(mesh):
    in_specs = (
        P("tok", ("row", "col")),
        P("row", ("col", "tok")),
        P("row", ("col", "tok")),
        P(("col", "tok"), "row"),
        P("tok", ("row", "col")),
    )
    out_specs = (
        P("tok", ("row", "col")),
        P("tok", ("row", "col")),
        P("row", ("col", "tok")),
        P("row", ("col", "tok")),
        P(("col", "tok"), "row"),
    )
    return jax.shard_map(local, mesh=mesh, in_specs=in_specs, out_specs=out_specs, check_vma=False)
```

profile of v0, /device:TPU:1, one launch (start us, length us, event | category | flops | bytes accessed | tf_op | source)
XLA Modules:
  0.0 635.9 jit_solution(7308681097724997905)
XLA Ops:
  7.2 0.7 all-gather.6.cloned.1.call-update
  8.0 0.7 all-gather.4.cloned.1.call-update
  8.7 0.7 all-gather.8.cloned.1.call-update
  9.5 23.2 %all_gather.15 = bf16[256,1024]{1,0:T(8,128)(2,1)S(1)} all-gather(bf16[256,128]{1,0:T(8,128)(2,1)S(1)} %copy-done.2), channel_id=1, replica_groups=mesh['tok'=4,'row'=8,'col'=8] {'col'}, dimensions={1}, use_global_device_ids=true | all-gather | bytes 589824 | tf_op jit(solution)/shard_map/all_gather | solution.py:34
  32.7 21.8 %all_gather.19 = bf16[256,1024]{1,0:T(8,128)(2,1)S(1)} all-gather(bf16[256,128]{1,0:T(8,128)(2,1)S(1)} %copy-done.3), channel_id=1, replica_groups=mesh['tok'=4,'row'=8,'col'=8] {'col'}, dimensions={1}, use_global_device_ids=true | all-gather | bytes 589824 | tf_op jit(solution)/shard_map/all_gather | solution.py:48
  54.5 5.6 all-gather.6.cloned.1.call-done
  60.2 4.5 fusion.2
  64.6 44.1 %all-gather.4.cloned.1.call-done = bf16[1024,1792]{0,1:T(8,128)(2,1)} async-done(((bf16[1024,448]{0,1:T(8,128)(2,1)}), bf16[1024,1792]{0,1:T(8,128)(2,1)}) %all-gather.4.cloned.1.call-update) | async-done | bytes 3670032 | tf_op jit(solution)/shard_map/all_gather | solution.py:36
  108.7 4.4 fusion.1
  113.2 44.2 %all-gather.8.cloned.1.call-done = bf16[1792,1024]{1,0:T(8,128)(2,1)} async-done(((bf16[448,1024]{1,0:T(8,128)(2,1)}), bf16[1792,1024]{1,0:T(8,128)(2,1)}) %all-gather.8.cloned.1.call-update) | async-done | bytes 3670032 | tf_op jit(solution)/shard_map/all_gather | solution.py:39
  157.4 4.4 fusion.4
  161.8 0.0 reduce-scatter.8.cloned.1.call-start
  161.9 141.6 %all-reduce.3.cloned.1.call-done = (f32[256,1792]{1,0:T(8,128)}, f32[256,1792]{1,0:T(8,128)}, f32[256,1792]{1,0:T(8,128)}) async-done(((f32[256,1792]{1,0:T(8,128)}, f32[256,1792]{1,0:T(8,128)}, f32[256,1792]{1,0:T(8,128)}), (f32[256,1792]{1,0:T(8,128)}, f32[256,1792]{1,0:T(8,128)}, f32[256,1792]{1,0:T(8,128)})) %all-reduce.3.cloned.1.call-update) | async-done | bytes 5505040 | tf_op jit(solution)/shard_map/psum | solution.py:42
  303.5 3.8 multiply_convert_fusion
  307.4 1.1 fusion.5
  308.5 0.9 copy-done.4
  309.4 2.2 convolution_add_fusion
  311.6 4.1 fusion.3
  315.8 4.2 convolution_bitcast_fusion
  320.1 4.1 convolution_bitcast_fusion.1
  324.2 1.0 copy-done.1
  325.2 4.1 fusion.6
  329.3 18.4 %reduce-scatter.8.cloned.1.call-done = f32[256,128]{1,0:T(8,128)} async-done(((f32[256,1024]{1,0:T(8,128)}), f32[256,128]{1,0:T(8,128)}) %reduce-scatter.8.cloned.1.call-update) | async-done | bytes 131088 | tf_op jit(solution)/shard_map/reduce_scatter | solution.py:53
  347.7 1.5 convert_element_type.28
  349.2 41.3 %reduce-scatter.6.cloned.1.call-done = f32[256,128]{1,0:T(8,128)} async-done(((f32[256,1024]{1,0:T(8,128)}), f32[256,128]{1,0:T(8,128)}) %reduce-scatter.6.cloned.1.call-update) | async-done | bytes 131088 | tf_op jit(solution)/shard_map/reduce_scatter | solution.py:45
  390.6 1.5 convert_element_type.25
  392.1 79.8 %reduce-scatter.12.cloned.1.call-done = f32[1024,448]{0,1:T(8,128)} async-done(((f32[1024,1792]{0,1:T(8,128)}), f32[1024,448]{0,1:T(8,128)}) %reduce-scatter.12.cloned.1.call-update) | async-done | bytes 1835024 | tf_op jit(solution)/shard_map/reduce_scatter | solution.py:60
  471.9 2.6 convert_element_type.30
  474.5 74.9 %reduce-scatter.10.cloned.1.call-done = f32[1024,448]{0,1:T(8,128)} async-done(((f32[1024,1792]{0,1:T(8,128)}), f32[1024,448]{0,1:T(8,128)}) %reduce-scatter.10.cloned.1.call-update) | async-done | bytes 1835024 | tf_op jit(solution)/shard_map/reduce_scatter | solution.py:57
  549.4 2.6 convert_element_type.29
  551.9 74.9 %reduce-scatter.14.cloned.1.call-done = f32[448,1024]{1,0:T(8,128)} async-done(((f32[1792,1024]{1,0:T(8,128)}), f32[448,1024]{1,0:T(8,128)}) %reduce-scatter.14.cloned.1.call-update) | async-done | bytes 1835024 | tf_op jit(solution)/shard_map/reduce_scatter | solution.py:64
  626.8 2.6 convert_element_type.31
  (24 shorter events, 0.4 us)
Async XLA Ops:
  7.2 2.3 copy-start.2
  7.2 25.5 %copy-start.3 = (bf16[256,128]{1,0:T(8,128)(2,1)S(1)}, bf16[256,128]{1,0:T(8,128)(2,1)}, u32[]{:S(2)}) copy-start(bf16[256,128]{1,0:T(8,128)(2,1)} %param.9) | copy-start | bytes 196612
  7.2 53.0 %all-gather.6.cloned.1.call-start = ((), (), s32[]{:S(2)}) async-start(), calls=%async_computation.6 | async-start | bytes 4587520 | tf_op jit(solution)/shard_map/all_gather | solution.py:37
  7.9 100.8 %all-gather.4.cloned.1.call-start = ((), (), s32[]{:S(2)}) async-start(), calls=%async_computation.5 | async-start | bytes 4587520 | tf_op jit(solution)/shard_map/all_gather | solution.py:36
  8.7 148.7 %all-gather.8.cloned.1.call-start = ((), (), s32[]{:S(2)}) async-start(), calls=%async_computation.7 | async-start | bytes 4587520 | tf_op jit(solution)/shard_map/all_gather | solution.py:39
  9.4 294.1 %all-reduce.3.cloned.1.call-start = ((), (), s32[]{:S(2)}) async-start(), calls=%async_computation.13 | async-start | bytes 11010048 | tf_op jit(solution)/shard_map/psum | solution.py:42
  54.5 102.8 %copy-start = (bf16[256,1024]{1,0:T(8,128)(2,1)}, bf16[256,1024]{1,0:T(8,128)(2,1)S(1)}, u32[]{:S(2)}) copy-start(bf16[256,1024]{1,0:T(8,128)(2,1)S(1)} %all_gather.19) | copy-start | bytes 1572868
  161.8 185.9 %reduce-scatter.8.cloned.1.call-start = ((), (), s32[]{:S(2)}) async-start(), calls=%async_computation.9 | async-start | bytes 1179648 | tf_op jit(solution)/shard_map/reduce_scatter | solution.py:53
  303.5 3.8 copy-start.5
  307.4 2.0 copy-start.4
  311.6 79.0 %reduce-scatter.6.cloned.1.call-start = ((), (), s32[]{:S(2)}) async-start(), calls=%async_computation.8 | async-start | bytes 1179648 | tf_op jit(solution)/shard_map/reduce_scatter | solution.py:45
  315.8 156.2 %reduce-scatter.12.cloned.1.call-start = ((), (), s32[]{:S(2)}) async-start(), calls=%async_computation.11 | async-start | bytes 9175040 | tf_op jit(solution)/shard_map/reduce_scatter | solution.py:60
  320.0 229.4 %reduce-scatter.10.cloned.1.call-start = ((), (), s32[]{:S(2)}) async-start(), calls=%async_computation.10 | async-start | bytes 9175040 | tf_op jit(solution)/shard_map/reduce_scatter | solution.py:57
  324.1 1.0 copy-start.1
  324.2 302.6 %reduce-scatter.14.cloned.1.call-start = ((), (), s32[]{:S(2)}) async-start(), calls=%async_computation.12 | async-start | bytes 9175040 | tf_op jit(solution)/shard_map/reduce_scatter | solution.py:64
Sparse Core Ops, SparseCore 0:
  9.8 50.2 all-gather.5
  62.0 46.7 all-gather.3
  110.6 46.7 all-gather.7
  161.9 141.5 all-reduce.2
  311.7 35.9 reduce-scatter.7
  350.1 40.4 reduce-scatter.5
  393.1 78.7 reduce-scatter.11
  474.5 74.8 reduce-scatter.9
  551.9 74.8 reduce-scatter.13
where the time goes:
time: 636 us
  waiting for transfers between devices  527 us (83%)
  blocking collectives  45.1 us (7%)
  matrix products  33.1 us (5%)
  other arithmetic  14.6 us (2%)
  between operations  13.9 us (2%)
    psum x1, waiting for transfers between devices, local(): gate_sum, up_sum = lax.psum((gate_part, up_part), 'row')  142 us
    reduce_scatter x1, waiting for transfers between devices, local(): lax.psum_scatter(contract_first(features, up_slope), 'tok', scatter_dimen...  79.8 us
    reduce_scatter x1, waiting for transfers between devices, local(): lax.psum_scatter(contract_first(hidden, cot_tile), 'tok', scatter_dimensi...  74.9 us
    reduce_scatter x1, waiting for transfers between devices, local(): lax.psum_scatter(contract_first(features, gate_slope), 'tok', scatter_dim...  74.9 us
    all_gather x1, waiting for transfers between devices, local(): down_tile = lax.all_gather(down_weight, 'tok', axis=0, tiled=True)  44.2 us
    all_gather x1, waiting for transfers between devices, local(): lax.all_gather(gate_weight, 'tok', axis=1, tiled=True)  44.1 us
    reduce_scatter x1, waiting for transfers between devices, local(): lax.psum_scatter(out_part, 'col', scatter_dimension=1, tiled=True)  41.3 us
    all_gather x1, blocking collectives, local(): features = lax.all_gather(tokens, 'col', axis=1, tiled=True)  23.2 us
  transfers between devices with their start and end apart: 9, of which 9 were waited for; matrix products, arithmetic and copies ran while one was open for 5% of the time, Pallas kernels for 0%

commit v1 on v0

v1 whole, which is shorter than its diff:
```python
import jax
import jax.numpy as jnp
from jax import lax
from jax.sharding import PartitionSpec as P


def contract_last(left_op, right_op):
    return lax.dot_general(
        left_op, right_op, (((1,), (1,)), ((), ())), preferred_element_type=jnp.float32
    )


def contract_first(left_op, right_op):
    return lax.dot_general(
        left_op, right_op, (((0,), (0,)), ((), ())), preferred_element_type=jnp.float32
    )


def gather_block(block):
    wide = lax.all_gather(block, "col", axis=1, tiled=True)
    return lax.all_gather(wide, "tok", axis=0, tiled=True)


def scatter_block(part):
    some = lax.psum_scatter(part, "tok", scatter_dimension=0, tiled=True)
    return lax.psum_scatter(some, "col", scatter_dimension=1, tiled=True).astype(jnp.bfloat16)


def local(tokens, gate_weight, up_weight, down_weight, cotangent):
    features = gather_block(tokens)
    cot = gather_block(cotangent)
    gate_up = jnp.concatenate([gate_weight, up_weight], axis=1)
    parts = jnp.dot(features, gate_up, preferred_element_type=jnp.float32)
    sums = lax.psum_scatter(parts, "row", scatter_dimension=0, tiled=True)
    slope_part = contract_last(cot, down_weight)
    slope = lax.psum_scatter(slope_part, "row", scatter_dimension=0, tiled=True)
    gate_sum, up_sum = jnp.split(sums, 2, axis=1)
    squash = jax.nn.sigmoid(gate_sum)
    swish = gate_sum * squash
    hidden = (swish * up_sum).astype(jnp.bfloat16)
    gate_slope = (slope * up_sum * squash * (1.0 + gate_sum * (1.0 - squash))).astype(jnp.bfloat16)
    up_slope = (slope * swish).astype(jnp.bfloat16)
    hidden = lax.all_gather(hidden, "row", axis=0, tiled=True)
    slopes = jnp.concatenate([gate_slope, up_slope], axis=1)
    slopes = lax.all_gather(slopes, "row", axis=0, tiled=True)
    block_out = scatter_block(jnp.dot(hidden, down_weight, preferred_element_type=jnp.float32))
    input_grad = scatter_block(contract_last(slopes, gate_up))
    grads = contract_first(features, slopes).astype(jnp.bfloat16)
    gate_grad, up_grad = jnp.split(grads, 2, axis=1)
    down_grad = contract_first(hidden, cot).astype(jnp.bfloat16)
    return block_out, input_grad, gate_grad, up_grad, down_grad


def solution(mesh):
    in_specs = (
        P("tok", ("row", "col")),
        P("row", ("col", "tok")),
        P("row", ("col", "tok")),
        P(("col", "tok"), "row"),
        P("tok", ("row", "col")),
    )
    out_specs = (
        P("tok", ("row", "col")),
        P("tok", ("row", "col")),
        P("row", ("col", "tok")),
        P("row", ("col", "tok")),
        P(("col", "tok"), "row"),
    )
    return jax.shard_map(local, mesh=mesh, in_specs=in_specs, out_specs=out_specs, check_vma=False)
```

time: 636 us -> 445 us (0.70)
  waiting for transfers between devices: 527 us -> 317 us
  blocking collectives: 45.1 us -> 74.8 us
  other arithmetic: 14.6 us -> 5.09 us
  matrix products: 33.1 us -> 25.6 us
    psum x1 -> x0, waiting for transfers between devices: 142 us -> none  [local(): gate_sum, up_sum = lax.psum((gate_part, up_part), 'row')]
    all_gather x3, waiting for transfers between devices: 93.9 us -> 52.3 us  [the longest x2 43.9 us: gather_block(): return lax.all_gather(wide, 'tok', axis=0, tiled=True)]
    all_gather x2 -> x3, blocking collectives: 45.1 us -> 74.8 us  [the longest x2 48.3 us: gather_block(): wide = lax.all_gather(block, 'col', axis=1, tiled=True)]
    reduce_scatter x5 -> x6, waiting for transfers between devices: 289 us -> 265 us  [the longest x2 98.1 us: scatter_block(): some = lax.psum_scatter(part, 'tok', scatter_dimension=0, tiled=True)]
    convert_element_type x6 -> x3, other arithmetic: 14.6 us -> 4.38 us  [the longest x2 3.08 us: scatter_block(): lax.psum_scatter(some, 'col', scatter_dimension=1, tiled=True)]
    dot_general x3 -> x2, matrix products: 12.3 us -> 5.85 us  [contract_first(): lax.dot_general(left_op, right_op, (((0,), (0,)), ((), ())), preferred_el...]
    dot_general x3 -> x2, matrix products: 13 us -> 9.3 us  [the longest x1 6.04 us: local(): parts = jnp.dot(features, gate_up, preferred_element_type=jnp.float32)]
  transfers between devices with their start and end apart: 9 -> 9, of which waited for: 9 -> 9; matrix products, arithmetic and copies ran while one was open for 5% -> 7% of each run, Pallas kernels for 0% -> 0%
where the time goes in v1:
time: 445 us; the launch traced here: 441 us
  waiting for transfers between devices  317 us (71%)
  blocking collectives  74.8 us (17%)
  matrix products  25.6 us (6%)
  between operations  13.9 us (3%)
  other arithmetic  5.09 us (1%)
  local copies, waits for them, and re-layouts  4.49 us (1%)
    reduce_scatter x2, waiting for transfers between devices, scatter_block(): some = lax.psum_scatter(part, 'tok', scatter_dimension=0, tiled=True)  98.1 us
    reduce_scatter x2, waiting for transfers between devices, scatter_block(): lax.psum_scatter(some, 'col', scatter_dimension=1, tiled=True)  73.3 us
    reduce_scatter x1, waiting for transfers between devices, local(): sums = lax.psum_scatter(parts, 'row', scatter_dimension=0, tiled=True)  56.1 us
    all_gather x2, blocking collectives, gather_block(): wide = lax.all_gather(block, 'col', axis=1, tiled=True)  48.3 us
    all_gather x2, waiting for transfers between devices, gather_block(): return lax.all_gather(wide, 'tok', axis=0, tiled=True)  43.9 us
    reduce_scatter x1, waiting for transfers between devices, local(): slope = lax.psum_scatter(slope_part, 'row', scatter_dimension=0, tiled=True)  37.1 us
    all_gather x1, blocking collectives, local(): hidden = lax.all_gather(hidden, 'row', axis=0, tiled=True)  26.5 us
    dot_general x2, matrix products, contract_last(): lax.dot_general(left_op, right_op, (((1,), (1,)), ((), ())), preferred_el...  10.4 us
  transfers between devices with their start and end apart: 9, of which 9 were waited for; matrix products, arithmetic and copies ran while one was open for 7% of the time, Pallas kernels for 0%

profile of v1, /device:TPU:1, one launch (start us, length us, event | category | flops | bytes accessed | tf_op | source)
XLA Modules:
  0.0 441.3 jit_solution(10508178719969974293)
XLA Ops:
  7.2 25.3 %all_gather.21 = bf16[256,1024]{1,0:T(8,128)(2,1)} all-gather(bf16[256,128]{1,0:T(8,128)(2,1)} %param.9), channel_id=1, replica_groups=mesh['tok'=4,'row'=8,'col'=8] {'col'}, dimensions={1}, use_global_device_ids=true | all-gather | bytes 589824 | tf_op jit(solution)/shard_map/all_gather | solution.py:20
  32.6 0.0 all-gather.4.cloned.1.call-start
  32.6 22.9 %all_gather.18 = bf16[256,1024]{1,0:T(8,128)(2,1)} all-gather(bf16[256,128]{1,0:T(8,128)(2,1)} %param.5), channel_id=1, replica_groups=mesh['tok'=4,'row'=8,'col'=8] {'col'}, dimensions={1}, use_global_device_ids=true | all-gather | bytes 589824 | tf_op jit(solution)/shard_map/all_gather | solution.py:20
  55.6 0.0 reduce-scatter.13.cloned.1.call-start
  55.6 15.8 %all-gather.6.cloned.1.call-done = bf16[1024,1024]{1,0:T(8,128)(2,1)} async-done(((bf16[256,1024]{1,0:T(8,128)(2,1)}), bf16[1024,1024]{1,0:T(8,128)(2,1)}) %all-gather.6.cloned.1.call-update) | async-done | bytes 2097168 | tf_op jit(solution)/shard_map/all_gather | solution.py:21
  71.4 4.0 fusion.3
  75.5 0.0 reduce-scatter.7.cloned.1.call-start
  75.5 1.1 copy-done.1
  76.6 1.0 constant_dynamic-update-slice_fusion.1
  77.6 1.0 constant_dynamic-update-slice_fusion
  78.6 28.1 %all-gather.4.cloned.1.call-done = bf16[1024,1024]{1,0:T(8,128)(2,1)} async-done(((bf16[256,1024]{1,0:T(8,128)(2,1)}), bf16[1024,1024]{1,0:T(8,128)(2,1)}) %all-gather.4.cloned.1.call-update) | async-done | bytes 2097168 | tf_op jit(solution)/shard_map/all_gather | solution.py:21
  106.7 6.0 %convolution_bitcast_fusion = f32[1024,896]{0,1:T(8,128)} fusion(bf16[1024,896]{0,1:T(8,128)(2,1)} %constant_dynamic-update-slice_fusion, bf16[1024,1024]{1,0:T(8,128)(2,1)} %all-gather.4.cloned.1.call-done), kind=kOutput, calls=%fused_computation | convolution fusion | flops 1879048192 | bytes 7602176 | tf_op jit(solution)/shard_map/dot_general | solution.py:33
  112.8 0.0 all-gather.8.cloned.1.call-start
  112.8 37.1 %reduce-scatter.13.cloned.1.call-done = f32[128,448]{0,1:T(8,128)} async-done(((f32[1024,448]{0,1:T(8,128)}), f32[128,448]{0,1:T(8,128)}) %reduce-scatter.13.cloned.1.call-update) | async-done | bytes 229392 | tf_op jit(solution)/shard_map/reduce_scatter | solution.py:36
  149.9 56.1 %reduce-scatter.7.cloned.1.call-done = f32[128,896]{0,1:T(8,128)} async-done(((f32[1024,896]{0,1:T(8,128)}), f32[128,896]{0,1:T(8,128)}) %reduce-scatter.7.cloned.1.call-update) | async-done | bytes 458768 | tf_op jit(solution)/shard_map/reduce_scatter | solution.py:34
  206.1 1.3 multiply_convert_fusion.1
  207.4 0.7 pad_maximum_fusion
  208.1 0.0 reduce-scatter.9.cloned.1.call-start
  208.1 26.5 %all_gather.20 = bf16[1024,448]{0,1:T(8,128)(2,1)S(1)} all-gather(bf16[128,448]{0,1:T(8,128)(2,1)S(1)} %get-tuple-element.9), channel_id=1, replica_groups=mesh['tok'=4,'row'=8,'col'=8] {'row'}, dimensions={0}, use_global_device_ids=true | all-gather | bytes 1032192 | tf_op jit(solution)/shard_map/all_gather | solution.py:43
  234.7 3.3 fusion.2
  238.0 0.0 reduce-scatter.15.cloned.1.call-start
  238.0 8.4 %all-gather.8.cloned.1.call-done = bf16[1024,896]{0,1:T(8,128)(2,1)} async-done(((bf16[128,896]{0,1:T(8,128)(2,1)}), bf16[1024,896]{0,1:T(8,128)(2,1)}) %all-gather.8.cloned.1.call-update) | async-done | bytes 1835024 | tf_op jit(solution)/shard_map/all_gather | solution.py:45
  246.4 6.4 %fusion.4 = f32[1024,1024]{1,0:T(8,128)} fusion(bf16[1024,896]{0,1:T(8,128)(2,1)} %all-gather.8.cloned.1.call-done, bf16[1024,896]{0,1:T(8,128)(2,1)} %constant_dynamic-update-slice_fusion), kind=kOutput, calls=%fused_computation.14 | convolution fusion | flops 1879048192 | bytes 7864320 | tf_op jit(solution)/shard_map/dot_general | solution.py:8
  252.9 46.3 %reduce-scatter.9.cloned.1.call-done = f32[256,1024]{1,0:T(8,128)} async-done(((f32[1024,1024]{1,0:T(8,128)}), f32[256,1024]{1,0:T(8,128)}) %reduce-scatter.9.cloned.1.call-update) | async-done | bytes 1048592 | tf_op jit(solution)/shard_map/reduce_scatter | solution.py:25
  299.3 51.8 %reduce-scatter.15.cloned.1.call-done = f32[256,1024]{1,0:T(8,128)} async-done(((f32[1024,1024]{1,0:T(8,128)}), f32[256,1024]{1,0:T(8,128)}) %reduce-scatter.15.cloned.1.call-update) | async-done | bytes 1048592 | tf_op jit(solution)/shard_map/reduce_scatter | solution.py:25
  351.1 3.8 convolution_convert_fusion
  354.9 2.1 convert_bitcast_fusion
  357.0 1.4 fusion.1
  358.4 31.8 %reduce-scatter.11.cloned.1.call-done = f32[256,128]{1,0:T(8,128)} async-done(((f32[256,1024]{1,0:T(8,128)}), f32[256,128]{1,0:T(8,128)}) %reduce-scatter.11.cloned.1.call-update) | async-done | bytes 131088 | tf_op jit(solution)/shard_map/reduce_scatter | solution.py:26
  390.1 1.5 convert_element_type.25
  391.7 41.5 %reduce-scatter.17.cloned.1.call-done = f32[256,128]{1,0:T(8,128)} async-done(((f32[256,1024]{1,0:T(8,128)}), f32[256,128]{1,0:T(8,128)}) %reduce-scatter.17.cloned.1.call-update) | async-done | bytes 131088 | tf_op jit(solution)/shard_map/reduce_scatter | solution.py:26
  433.2 1.5 convert_element_type.28
  (21 shorter events, 0.3 us)
Async XLA Ops:
  7.2 64.2 %copy-start = (bf16[448,1024]{1,0:T(8,128)(2,1)S(1)}, bf16[448,1024]{1,0:T(8,128)(2,1)}, u32[]{:S(2)}) copy-start(bf16[448,1024]{1,0:T(8,128)(2,1)} %param.8) | copy-start | bytes 2752516
  7.2 64.2 %all-gather.6.cloned.1.call-start = ((), (), s32[]{:S(2)}) async-start(), calls=%async_computation.10 | async-start | bytes 2621440 | tf_op jit(solution)/shard_map/all_gather | solution.py:21
  32.6 74.1 %all-gather.4.cloned.1.call-start = ((), (), s32[]{:S(2)}) async-start(), calls=%async_computation.6 | async-start | bytes 2621440 | tf_op jit(solution)/shard_map/all_gather | solution.py:21
  55.6 94.3 %reduce-scatter.13.cloned.1.call-start = ((), (), s32[]{:S(2)}) async-start(), calls=%async_computation.11 | async-start | bytes 2064384 | tf_op jit(solution)/shard_map/reduce_scatter | solution.py:36
  75.4 1.2 copy-start.1
  75.4 2.2 copy-start.2
  75.5 130.6 %reduce-scatter.7.cloned.1.call-start = ((), (), s32[]{:S(2)}) async-start(), calls=%async_computation.7 | async-start | bytes 4128768 | tf_op jit(solution)/shard_map/reduce_scatter | solution.py:34
  112.8 133.7 %all-gather.8.cloned.1.call-start = ((), (), s32[]{:S(2)}) async-start(), calls=%async_computation.12 | async-start | bytes 2064384 | tf_op jit(solution)/shard_map/all_gather | solution.py:45
  208.1 91.1 %reduce-scatter.9.cloned.1.call-start = ((), (), s32[]{:S(2)}) async-start(), calls=%async_computation.8 | async-start | bytes 5242880 | tf_op jit(solution)/shard_map/reduce_scatter | solution.py:25
  238.0 113.1 %reduce-scatter.15.cloned.1.call-start = ((), (), s32[]{:S(2)}) async-start(), calls=%async_computation.13 | async-start | bytes 5242880 | tf_op jit(solution)/shard_map/reduce_scatter | solution.py:25
  252.9 137.3 %reduce-scatter.11.cloned.1.call-start = ((), (), s32[]{:S(2)}) async-start(), calls=%async_computation.9 | async-start | bytes 1179648 | tf_op jit(solution)/shard_map/reduce_scatter | solution.py:26
  299.2 134.0 %reduce-scatter.17.cloned.1.call-start = ((), (), s32[]{:S(2)}) async-start(), calls=%async_computation.14 | async-start | bytes 1179648 | tf_op jit(solution)/shard_map/reduce_scatter | solution.py:26
  351.1 3.8 copy-start.3
  351.1 3.8 copy-start.4
Sparse Core Ops, SparseCore 0:
  32.7 38.6 all-gather.5
  73.2 33.4 all-gather.3
  109.3 40.6 reduce-scatter.12
  152.3 53.6 reduce-scatter.6
  208.3 38.0 all-gather.7
  248.8 50.3 reduce-scatter.8
  301.9 49.1 reduce-scatter.14
  353.6 36.4 reduce-scatter.10
  392.7 40.4 reduce-scatter.16

commit v2 on v1

v2 whole, which is shorter than its diff:
```python
from types import SimpleNamespace

import math

import jax
import jax.numpy as jnp
from jax import lax
from jax.experimental import pallas as pl
from jax.experimental.pallas import tpu as pltpu
from jax.sharding import PartitionSpec as P

BF, F32 = jnp.bfloat16, jnp.float32
MESH = pl.DeviceIdType.MESH
SENDS = 103
VMEM_LIMIT = 60 * 2 ** 20
POOL = 32


def dot(a, b):
    return jnp.dot(a, b, preferred_element_type=F32)


def dot_t(a, b):
    return lax.dot_general(a, b, (((1,), (1,)), ((), ())), preferred_element_type=F32)


class Scatter:
    NAMES = ("part", "sy3", "yr3", "sy2", "yr2", "sx1", "xr1", "sx2", "xr2", "sb", "br3", "br2",
             "sd", "rd", "fin", "zlr")

    @staticmethod
    def shapes(fs, ct):
        h = fs // 2
        v = pltpu.VMEM
        return [
            v((4, 2, 4, fs, ct), F32),
            v((2, 4, h, ct), BF), v((2, 4, h, ct), BF),
            v((2, 2, 4, h, ct), BF), v((2, 2, 4, h, ct), BF),
            v((4, 2, h, ct), BF), v((4, 2, h, ct), BF),
            v((4, 2, 2, h, ct), BF), v((4, 2, 2, h, ct), BF),
            v((4, 2, h, ct), F32),
            v((2, h, ct), F32), v((2, 2, h, ct), F32),
            v((4, 3, h, ct), BF), v((4, 3, h, ct), BF),
            v((2, fs, ct), F32), v((fs, ct), F32),
        ]

    def __init__(self, refs):
        for name, ref in zip(self.NAMES, refs):
            setattr(self, name, ref)


def kernel(tok_hbm, gw_hbm, uw_hbm, dw_hbm, cot_hbm,
           out_ref, inp_ref, gg_ref, ug_ref, dg_ref, *scratch):
    n_sc = len(Scatter.NAMES)
    (tok_ref, cot_ref, gw, uw, dw, gut, dwt, xt, ct, gu_part, gu_recv, gu_s1, gu_r1, gu_s2, gu_r2,
     sl_part, sl_recv, sl_s1, sl_r1, sl_s2, sl_r2, swish_ref, deriv_ref, hid, slo,
     *rest) = scratch
    so, si = Scatter(rest[:n_sc]), Scatter(rest[n_sc:2 * n_sc])
    grads, most, acts_out, wsem, send_sem, recv_sem = rest[2 * n_sc:]

    y, row, col = lax.axis_index("tok"), lax.axis_index("row"), lax.axis_index("col")
    z, c, zl, x = row // 2, row % 2, col // 4, col % 4
    zo = 1 - zl
    wrap = lambda v: lax.rem(v + 4, 4)
    xp1, xm1, xp2 = wrap(x + 1), wrap(x - 1), wrap(x + 2)
    zp1, zm1, zp2 = wrap(z + 1), wrap(z - 1), wrap(z + 2)
    XP, XM = (y, row, zl * 4 + xp1), (y, row, zl * 4 + xm1)
    X2 = (y, row, zl * 4 + xp2)
    Z2 = (y, zp2 * 2 + c, col)
    YP, YM = (wrap(y + 1), row, col), (wrap(y - 1), row, col)
    ZP, ZM = (y, zp1 * 2 + c, col), (y, zm1 * 2 + c, col)
    ZL, CORE = (y, row, (1 - zl) * 4 + x), (y, z * 2 + 1 - c, col)

    fs = tok_ref.shape[1]
    h = fs // 2
    A, B = pl.ds(0, h), pl.ds(h, h)
    ff = dw.shape[0]
    fq = ff // 4
    depth = gw.shape[0]

    copies, due = [], []

    def fresh():
        due.append(0)
        return len(due) - 1

    def send(src, dst, device, n=None):
        n = fresh() if n is None else n
        m = len(copies)
        if m >= POOL:
            copies[m - POOL].wait_send()
        cp = pltpu.make_async_remote_copy(
            src_ref=src, dst_ref=dst, send_sem=send_sem.at[m % POOL], recv_sem=recv_sem.at[n],
            device_id=device, device_id_type=MESH)
        cp.start()
        copies.append(cp)
        due[n] += math.prod(dst.shape) * dst.dtype.itemsize
        return cp

    def take(n, like):
        assert math.prod(like.shape) * like.dtype.itemsize == due[n]
        pltpu.make_async_remote_copy(
            src_ref=like, dst_ref=like, send_sem=send_sem.at[0], recv_sem=recv_sem.at[n],
            device_id=XP, device_id_type=MESH).wait_recv()

    loads = [pltpu.make_async_copy(s, d, wsem.at[i])
             for i, (s, d) in enumerate((
                 (gw_hbm, gut.at[:, 0]), (uw_hbm, gut.at[:, 1]), (dw_hbm, dw)))]
    acts = [pltpu.make_async_copy(s, d, wsem.at[6 + i])
            for i, (s, d) in enumerate(((tok_hbm, tok_ref), (cot_hbm, cot_ref)))]
    for cp in acts + loads:
        cp.start()
    barrier = pltpu.get_barrier_semaphore()
    for device in (XP, XM, X2, YP, YM, ZP, ZM, Z2, ZL, CORE):
        pl.semaphore_signal(barrier, inc=1, device_id=device, device_id_type=MESH)
    for cp in acts:
        cp.wait()
    xt[0, zl, x] = tok_ref[...].T
    ct[0, zl, x] = cot_ref[...].T
    pl.semaphore_wait(barrier, 10)

    def gather(v):
        k = {}
        gx, g2, gy = fresh(), fresh(), fresh()

        def spread(blk, far2, far1, *yps):
            send(blk, blk, XP, gx)
            send(blk, blk, XM, gx)
            yp = send(blk, far2, YP, *yps)
            send(blk, far1, YM, gy)
            send(blk, blk, X2, g2)
            return yp

        def s0():
            k["zl"] = send(v.at[0, zl, x], v.at[0, zl, x], ZL)
            k["yp"] = spread(v.at[0, zl, x], v.at[2, zl, x], v.at[1, zl, x])

        def s1():
            k["zl"].wait_recv()
            spread(v.at[0, zo, x], v.at[2, zo, x], v.at[1, zo, x], gy)

        def s1y():
            k["yp"].wait_recv()
            k["yf"] = fresh()
            send(v.at[2, zl, x], v.at[3, zl, x], YP, k["yf"])

        def ysend(xi, n):
            blk = v.at[0, :, xi, A]
            send(blk, v.at[2, :, xi, A], YP, n)
            send(blk, v.at[1, :, xi, A], YM, n)

        def s2():
            take(gx, v.at[0, :, pl.ds(0, 2)])
            k["a"] = fresh()
            ysend(xm1, k["a"])
            ysend(xp1, k["a"])

        def xsend(s, n):
            blk = v.at[s, :, x, B]
            send(blk, blk, XP, n)
            send(blk, blk, XM, n)

        def xfwd(s, n):
            send(v.at[s, 0, xm1, B], v.at[s, 0, xm1, B], XP, n)
            send(v.at[s, 1, xp1, B], v.at[s, 1, xp1, B], XM, n)

        def s2b():
            take(gy, v.at[0, 0, pl.ds(0, 3)])
            send(v.at[1, zo, x], v.at[3, zo, x], YM, k["yf"])
            k["x"] = fresh()
            xsend(2, k["x"])
            xsend(1, k["x"])

        def s3():
            take(g2, v.at[0, :, 0])
            ysend(xp2, k["a"])

        def s4():
            take(k["x"], v.at[0, :, pl.ds(0, 2)])
            k["xf"] = fresh()
            xfwd(1, k["xf"])
            xfwd(2, k["xf"])

        def s4b():
            take(k["yf"], v.at[0, :, 0])
            k["x3"] = fresh()
            xsend(3, k["x3"])

        def s5():
            take(k["a"], v.at[0, :, pl.ds(0, 3)])
            k["e"] = fresh()
            for xi in (xm1, xp1, xp2):
                send(v.at[2, 0, xi, A], v.at[3, 0, xi, A], YP, k["e"])
                send(v.at[1, 1, xi, A], v.at[3, 1, xi, A], YM, k["e"])

        def s6():
            take(k["xf"], v.at[0, 0, pl.ds(0, 2)])

        def s7():
            take(k["x3"], v.at[0, :, 0])
            k["xf3"] = fresh()
            xfwd(3, k["xf3"])

        def s8():
            take(k["e"], v.at[0, 0, pl.ds(0, 3)])
            take(k["xf3"], v.at[0, 0, 0])

        return SimpleNamespace(s0=s0, s1=s1, s1y=s1y, s2=s2, s2b=s2b, s3=s3, s4=s4, s4b=s4b, s5=s5, s6=s6, s7=s7, s8=s8)

    def row_sum(compute, finish, part, recv, s1, r1, s2, r2, cut):
        k = {}
        rows = part.shape[3]
        top, low = pl.ds(0, cut), pl.ds(cut, rows - cut)

        def chip(i, q, rs):
            return part[i, c, q, rs] + recv[i, q, rs]

        def a(i):
            total = compute(i)
            part[i, 0] = total[:, :128].reshape(part.shape[2:])
            part[i, 1] = total[:, 128:].reshape(part.shape[2:])
            k["c", i] = send(part.at[i, 1 - c], recv.at[i], CORE)

        def b(i):
            k["c", i].wait_recv()
            s1[i, top] = chip(i, zp2, top).astype(BF)
            s1[i, low] = chip(i, zp2, low).astype(BF)
            k["t", i] = fresh()
            send(s1.at[i, top], r1.at[i, top], ZP, k["t", i])
            send(s1.at[i, low], r1.at[i, low], ZM, k["t", i])

        def cc(i):
            s2[i, 0, low] = chip(i, zp1, low).astype(BF)
            s2[i, 1, top] = chip(i, zm1, top).astype(BF)
            take(k["t", i], r1.at[i])
            k["p", i] = fresh()
            s2[i, 0, top] = (chip(i, zp1, top) + r1[i, top].astype(F32)).astype(BF)
            send(s2.at[i, 0], r2.at[i, 0], ZP, k["p", i])
            s2[i, 1, low] = (chip(i, zm1, low) + r1[i, low].astype(F32)).astype(BF)
            send(s2.at[i, 1], r2.at[i, 1], ZM, k["p", i])

        def d(i):
            take(k["p", i], r2.at[i])
            full = pl.ds(0, rows)
            finish(i, chip(i, z, full) + (r2[i, 0].astype(F32) + r2[i, 1].astype(F32)))

        return SimpleNamespace(a=a, b=b, c=cc, d=d)

    def row_gather(block, first, second, whole, pair, direct=()):
        k = {}

        def a(i):
            k["p", i] = fresh()
            send(block(i, z), block(i, z), ZP, k["p", i])
            send(block(i, z), block(i, z), ZM, k["p", i])
            if i in direct:
                k["f", i] = send(block(i, z), block(i, z), Z2, k["p", i])

        def b(i):
            if i in direct:
                return
            take(k["p", i], pair(i))
            k["f", i] = fresh()
            send(first(i, zm1), first(i, zm1), ZP, k["f", i])
            send(second(i, zp1), second(i, zp1), ZM, k["f", i])

        def cc(i):
            if i in direct:
                take(k["p", i], pair(i, 3))
            else:
                take(k["f", i], block(i, 0))
            k["c", i] = send(whole(i), whole(i), CORE)

        def d(i):
            k["c", i].wait_recv()

        return SimpleNamespace(a=a, b=b, c=cc, d=d)

    def scatter(s, compute, n, ref):
        k = {}
        gy, gb = fresh(), fresh()

        def part(i):
            s.part[i] = compute(i).reshape(s.part.shape[1:])

        def x1(i):
            s.sx1[i] = s.part[i, :, xp2, B].astype(BF)
            k["x1", i] = fresh()
            send(s.sx1.at[i, 0], s.xr1.at[i, 0], XP, k["x1", i])
            send(s.sx1.at[i, 1], s.xr1.at[i, 1], XM, k["x1", i])

        def x2(i):
            take(k["x1", i], s.xr1.at[i])
            k["x2", i] = fresh()
            s.sx2[i, 0, 0] = (s.part[i, 0, xp1, B] + s.xr1[i, 0].astype(F32)).astype(BF)
            s.sx2[i, 0, 1] = s.part[i, 1, xp1, B].astype(BF)
            send(s.sx2.at[i, 0], s.xr2.at[i, 0], XP, k["x2", i])
            s.sx2[i, 1, 0] = s.part[i, 0, xm1, B].astype(BF)
            s.sx2[i, 1, 1] = (s.part[i, 1, xm1, B] + s.xr1[i, 1].astype(F32)).astype(BF)
            send(s.sx2.at[i, 1], s.xr2.at[i, 1], XM, k["x2", i])

        def x3(i):
            take(k["x2", i], s.xr2.at[i])
            s.sb[i] = s.part[i, :, x, B] + (s.xr2[i, 0].astype(F32) + s.xr2[i, 1].astype(F32))

        def y1():
            s.sy3[...] = s.part[3, :, :, A].astype(BF)
            k["y1p"] = send(s.sy3.at[0], s.yr3.at[0], YP)
            k["y1m"] = send(s.sy3.at[1], s.yr3.at[1], YM)

        def y2p():
            s.sy2[0, 1] = s.part[1, 1, :, A].astype(BF)
            k["y1p"].wait_recv()
            s.sy2[0, 0] = (s.part[1, 0, :, A] + s.yr3[0].astype(F32)).astype(BF)
            send(s.sy2.at[0], s.yr2.at[0], YP, gy)

        def y2m():
            s.sy2[1, 0] = s.part[2, 0, :, A].astype(BF)
            k["y1m"].wait_recv()
            s.sy2[1, 1] = (s.part[2, 1, :, A] + s.yr3[1].astype(F32)).astype(BF)
            send(s.sy2.at[1], s.yr2.at[1], YM, gy)

        def xsend(name, n, blk):
            k[name] = fresh()
            for d, (xi, device) in enumerate(((xp1, XP), (xm1, XM), (xp2, X2))):
                s.sd[n, d] = blk(xi).astype(BF)
                send(s.sd.at[n, d], s.rd.at[n, d], device, k[name])

        def xtake(name, n, blk):
            take(k[name], s.rd.at[n])
            return blk(x) + (s.rd[n, 0].astype(F32) + s.rd[n, 1].astype(F32) + s.rd[n, 2].astype(F32))

        def ablk(p):
            return lambda xi: s.part[0, p, xi, A] + (s.yr2[0, p, xi].astype(F32) + s.yr2[1, p, xi].astype(F32))

        def cblk(p):
            return lambda xi: s.part[0, p, xi, B]

        def a1q():
            take(gy, s.yr2)
            xsend("aq", 0, ablk(zo))

        def a1o():
            xsend("ao", 1, ablk(zl))

        def c1q():
            xsend("cq", 2, cblk(zo))

        def c1o():
            xsend("co", 3, cblk(zl))

        def a3q():
            s.fin[zo, A] = xtake("aq", 0, ablk(zo))

        def a3o():
            s.fin[zl, A] = xtake("ao", 1, ablk(zl))

        def c3q():
            s.fin[zo, B] = xtake("cq", 2, cblk(zo)) + (s.br2[0, zo] + s.br2[1, zo])

        def c3o():
            s.fin[zl, B] = xtake("co", 3, cblk(zl)) + (s.br2[0, zl] + s.br2[1, zl])

        def b1():
            k["b1"] = fresh()
            send(s.sb.at[3, 0], s.br3.at[0], YP, k["b1"])
            send(s.sb.at[3, 1], s.br3.at[1], YM, k["b1"])

        def b2():
            take(k["b1"], s.br3)
            s.sb[1, 0] = s.sb[1, 0] + s.br3[0]
            send(s.sb.at[1], s.br2.at[0], YP, gb)
            s.sb[2, 1] = s.sb[2, 1] + s.br3[1]
            send(s.sb.at[2], s.br2.at[1], YM, gb)

        def b3():
            take(gb, s.br2)

        def f1():
            k["f"] = send(s.fin.at[zo], s.zlr, ZL)

        def f2():
            k["f"].wait_recv()
            acts_out[n] = (s.fin[zl] + s.zlr[...]).T.astype(BF)
            cp = pltpu.make_async_copy(acts_out.at[n], ref, wsem.at[8 + n])
            cp.start()
            loads.append(cp)

        return SimpleNamespace(part=part, x1=x1, x2=x2, x3=x3, y1=y1, y2p=y2p, y2m=y2m, a1q=a1q, a1o=a1o,
                    a3q=a3q, a3o=a3o, c1q=c1q, c1o=c1o, c3q=c3q, c3o=c3o,
                    b1=b1, b2=b2, b3=b3, f1=f1, f2=f2)

    def chunk(v, i):
        return v[i].reshape(depth, v.shape[-1])

    def act(i, total):
        gate, up = total[:fq], total[fq:]
        squash = 1.0 / (1.0 + jnp.exp(-gate))
        swish = gate * squash
        swish_ref[i] = swish
        deriv_ref[i] = up * squash * (1.0 + gate * (1.0 - squash))
        hid[i, c, z] = (swish * up).astype(BF)

    def slopes(i, total):
        slo[i, c, 0, z] = (total * deriv_ref[i]).astype(BF)
        slo[i, c, 1, z] = (total * swish_ref[i]).astype(BF)

    def hidden_of(i):
        return jnp.concatenate([hid[i, j].reshape(ff, 128) for j in range(2)], axis=1)

    def slope_of(i, g):
        return jnp.concatenate([slo[i, j, g].reshape(ff, 128) for j in range(2)], axis=1)

    X, C = gather(xt), gather(ct)
    GU = row_sum(lambda i: dot(gut[...].reshape(2 * ff, depth), chunk(xt, i)), act,
                 gu_part, gu_recv, gu_s1, gu_r1, gu_s2, gu_r2, fq)
    S = row_sum(lambda i: dot(dw[...], chunk(ct, i)), slopes,
                sl_part, sl_recv, sl_s1, sl_r1, sl_s2, sl_r2, 64)
    H = row_gather(lambda i, q: hid.at[i, c, q],
                   lambda i, q: hid.at[i, c, q, pl.ds(0, 64)],
                   lambda i, q: hid.at[i, c, q, pl.ds(64, fq - 64)],
                   lambda i: hid.at[i, c], lambda i, n=2: hid.at[i, c, pl.ds(0, n)])
    G = row_gather(lambda i, q: slo.at[i, c, :, q],
                   lambda i, q: slo.at[i, c, 0, q],
                   lambda i, q: slo.at[i, c, 1, q],
                   lambda i: slo.at[i, c], lambda i, n=2: slo.at[i, c, :, pl.ds(0, n)], (0,))
    O = scatter(so, lambda i: dot(dwt[...], hidden_of(i)), 0, out_ref)
    I = scatter(si, lambda i: dot(gw[...], slope_of(i, 0)) + dot(uw[...], slope_of(i, 1)), 1, inp_ref)

    def wait_gate_up():
        for cp in loads[:2]:
            cp.wait()

    def turn_gate_up():
        for g, w in enumerate((gw, uw)):
            w[...] = gut[:, g].reshape(ff, depth).T

    def turn_down():
        loads[2].wait()
        dwt[...] = dw[...].T

    def leave(n, ref):
        cp = pltpu.make_async_copy(grads.at[n], ref, wsem.at[3 + n])
        cp.start()
        loads.append(cp)

    def down_grad():
        total = dot_t(hidden_of(0), chunk(ct, 0))
        for i in range(1, 4):
            total += dot_t(hidden_of(i), chunk(ct, i))
        grads[2] = total.astype(BF)
        leave(2, dg_ref)

    def most_grad(g):
        total = dot_t(slope_of(3, g), chunk(xt, 3))
        for i in (2, 1):
            total += dot_t(slope_of(i, g), chunk(xt, i))
        most[g] = total

    def weight_grad(ref, g):
        grads[g] = (most[g] + dot_t(slope_of(0, g), chunk(xt, 0))).astype(BF)
        leave(g, ref)

    X.s0(); wait_gate_up(); turn_gate_up(); turn_down(); X.s1(); X.s1y(); X.s2b(); X.s2(); X.s3(); C.s0()
    GU.a(0); GU.b(0); X.s4(); X.s4b(); C.s1(); C.s1y(); X.s5(); GU.c(0); X.s6(); GU.a(2); X.s7(); C.s2b()
    GU.a(1); GU.b(2); C.s2(); C.s3(); X.s8(); GU.b(1); GU.d(0); C.s4b(); H.a(0); GU.a(3); GU.c(2); C.s4()
    GU.b(3); GU.c(1); C.s7(); C.s5(); H.b(0); C.s6(); S.a(1); S.a(2); GU.d(2); GU.c(3); S.b(2); C.s8()
    H.a(2); S.a(3); H.c(0); S.b(3); H.d(0); S.b(1); O.part(0); GU.d(3); H.a(3); GU.d(1); H.a(1); O.c1o()
    S.c(3); H.b(2); H.b(3); S.c(2); S.a(0); O.c1q(); S.c(1); S.d(3); G.a(3); H.b(1); H.c(2); H.c(3); H.d(2)
    S.d(2); G.a(2); H.d(3); O.part(3); O.x1(3); O.y1(); O.part(2); O.x1(2); G.b(3); S.b(0); O.x2(3); H.c(1)
    S.d(1); G.a(1); O.x2(2); H.d(1); O.part(1); O.y2p(); O.y2m(); G.c(3); O.x3(3); G.b(2); S.c(0); O.x1(1)
    G.d(3); I.part(3); I.x1(3); G.b(1); O.x3(2); I.y1(); O.x2(1); G.c(2); O.b1(); I.x2(3); S.d(0); G.a(0)
    G.d(2); G.c(1); I.part(2); I.x1(2); G.d(1); I.part(1); I.x3(3); I.b1(); I.y2p(); O.x3(1); I.y2m()
    I.x1(1); O.a1q(); I.x2(2); most_grad(0); O.b2(); G.b(0); I.x2(1); G.c(0); O.a1o(); G.d(0); I.part(0)
    I.c1q(); I.x3(2); O.a3q(); I.x3(1); I.b2(); I.a1q(); weight_grad(gg_ref, 0); I.c1o(); I.a1o(); O.a3o()
    O.b3(); O.c3q(); O.f1(); most_grad(1); O.c3o(); I.a3q(); I.b3(); I.c3q(); I.f1(); I.c3o(); down_grad()
    weight_grad(ug_ref, 1); I.a3o(); O.f2(); I.f2()
    for cp in copies[-POOL:]:
        cp.wait_send()
    for cp in loads[3:]:
        cp.wait()


def publish_kernel(*refs):
    n = (len(refs) - 2) // 3
    src, dst, mid, (isem, osem) = refs[:n], refs[n:2 * n], refs[2 * n:3 * n], refs[3 * n:]
    ins = [pltpu.make_async_copy(src[i], mid[i], isem.at[i]) for i in range(n)]
    outs = [pltpu.make_async_copy(mid[i], dst[i], osem.at[i]) for i in range(n)]
    for cp in ins:
        cp.start()
    for cp, out in zip(ins, outs):
        cp.wait()
        out.start()
    for out in outs:
        out.wait()


def publish(arrays):
    n = len(arrays)
    hbm = pl.BlockSpec(memory_space=pltpu.HBM)
    sem = pltpu.SemaphoreType.DMA((n,))
    return pl.pallas_call(
        publish_kernel,
        out_shape=[jax.ShapeDtypeStruct(a.shape, a.dtype) for a in arrays],
        in_specs=[hbm] * n,
        out_specs=[hbm] * n,
        scratch_shapes=[*(pltpu.VMEM(a.shape, a.dtype) for a in arrays), sem, sem],
        compiler_params=pltpu.CompilerParams(vmem_limit_bytes=VMEM_LIMIT),
    )(*arrays)


def local(tokens, gate_weight, up_weight, down_weight, cotangent):
    ct, fs = tokens.shape
    depth, ff = gate_weight.shape
    fq = ff // 4
    v = pltpu.VMEM
    scratch = [
        v((ct, fs), BF), v((ct, fs), BF),
        v((depth, ff), BF), v((depth, ff), BF), v((ff, depth), BF),
        v((4, 2, fq, depth), BF), v((depth, ff), BF),
        v((4, 2, 4, fs, ct), BF), v((4, 2, 4, fs, ct), BF),
        v((4, 2, 4, 2 * fq, 128), F32), v((4, 4, 2 * fq, 128), F32),
        v((4, 2 * fq, 128), BF), v((4, 2 * fq, 128), BF),
        v((4, 2, 2 * fq, 128), BF), v((4, 2, 2 * fq, 128), BF),
        v((4, 2, 4, fq, 128), F32), v((4, 4, fq, 128), F32),
        v((4, fq, 128), BF), v((4, fq, 128), BF),
        v((4, 2, fq, 128), BF), v((4, 2, fq, 128), BF),
        v((4, fq, 128), F32), v((4, fq, 128), F32),
        v((4, 2, 4, fq, 128), BF), v((4, 2, 2, 4, fq, 128), BF),
        *Scatter.shapes(fs, ct), *Scatter.shapes(fs, ct),
        v((3, ff, depth), BF), v((2, ff, depth), F32), v((2, ct, fs), BF),
        pltpu.SemaphoreType.DMA((10,)),
        pltpu.SemaphoreType.DMA((POOL,)), pltpu.SemaphoreType.DMA((SENDS,)),
    ]
    hbm = pl.BlockSpec(memory_space=pltpu.HBM)
    sds = jax.ShapeDtypeStruct
    results = pl.pallas_call(
        kernel,
        out_shape=[sds((ct, fs), BF), sds((ct, fs), BF), sds((ff, depth), BF),
                   sds((ff, depth), BF), sds((ff, depth), BF)],
        in_specs=[hbm] * 5,
        out_specs=[hbm] * 5,
        scratch_shapes=scratch,
        compiler_params=pltpu.CompilerParams(
            collective_id=0, has_side_effects=True, vmem_limit_bytes=VMEM_LIMIT),
    )(tokens, gate_weight.T.reshape(4, fq, depth), up_weight.T.reshape(4, fq, depth), down_weight, cotangent)
    block_out, input_grad, gate_grad, up_grad, down_grad = publish(results)
    return block_out, input_grad, gate_grad.T, up_grad.T, down_grad


def solution(mesh):
    in_specs = (
        P("tok", ("row", "col")),
        P("row", ("col", "tok")),
        P("row", ("col", "tok")),
        P(("col", "tok"), "row"),
        P("tok", ("row", "col")),
    )
    out_specs = (
        P("tok", ("row", "col")),
        P("tok", ("row", "col")),
        P("row", ("col", "tok")),
        P("row", ("col", "tok")),
        P(("col", "tok"), "row"),
    )
    return jax.shard_map(local, mesh=mesh, in_specs=in_specs, out_specs=out_specs, check_vma=False)
```

time: 445 us -> 101 us (0.23)
  waiting for transfers between devices: 317 us -> 0 us
  Pallas kernels: 0 us -> 99.3 us
  blocking collectives: 74.8 us -> 0 us
  matrix products: 25.6 us -> 0 us
  between operations: 13.9 us -> 0.8 us
  other arithmetic: 5.09 us -> 0 us
  local copies, waits for them, and re-layouts: 4.49 us -> 0 us
    reduce_scatter x6 -> x0, waiting for transfers between devices: 265 us -> none  [the longest x2 98.1 us: scatter_block(): some = lax.psum_scatter(part, 'tok', scatter_dimension=0, tiled=True)]
    pallas_call x0 -> x2, Pallas kernels: none -> 99.3 us  [the longest x1 96.4 us: local(): pl.pallas_call(kernel, out_shape=[sds((ct, fs), BF), sds((ct, fs), BF), s...]
    all_gather x3 -> x0, blocking collectives: 74.8 us -> none  [the longest x2 48.3 us: gather_block(): wide = lax.all_gather(block, 'col', axis=1, tiled=True)]
    all_gather x3 -> x0, waiting for transfers between devices: 52.3 us -> none  [the longest x2 43.9 us: gather_block(): return lax.all_gather(wide, 'tok', axis=0, tiled=True)]
    dot_general x6 -> x0, matrix products: 25.6 us -> none  [the longest x2 10.4 us: contract_last(): lax.dot_general(left_op, right_op, (((1,), (1,)), ((), ())), preferred_el...]
  transfers between devices with their start and end apart: 9 -> 0, of which waited for: 9 -> 0; matrix products, arithmetic and copies ran while one was open for 7% -> 0% of each run, Pallas kernels for 0% -> 0%
where the time goes in v2:
time: 101 us; the launch traced here: 100 us
  Pallas kernels  99.3 us (98%)
    pallas_call x1, Pallas kernels, local(): pl.pallas_call(kernel, out_shape=[sds((ct, fs), BF), sds((ct, fs), BF), s...  96.4 us
    pallas_call x1, Pallas kernels, publish(): pl.pallas_call(publish_kernel, out_shape=[jax.ShapeDtypeStruct(a.shape, a...  2.87 us

profile of v2, /device:TPU:1, one launch (start us, length us, event | category | flops | bytes accessed | tf_op | source)
XLA Modules:
  0.0 100.1 jit_solution(17647162098157379369)
XLA Ops:
  0.6 96.4 %shard_map.92 = (bf16[256,128]{1,0:T(8,128)(2,1)}, bf16[256,128]{1,0:T(8,128)(2,1)}, bf16[448,1024]{1,0:T(8,128)(2,1)}, bf16[448,1024]{1,0:T(8,128)(2,1)}, bf16[448,1024]{1,0:T(8,128)(2,1)}) custom-call(bf16[256,128]{1,0:T(8,128)(2,1)} %tok_hbm.1, bf16[4,112,1024]{2,1,0:T(8,128)(2,1)} %bitcast.8, bf16[4,112,1024]{2,1,0:T(8,128)(2,1)} %bitcast.9, ...), custom_call_target="tpu_custom_call" | custom-call | tf_op jit(solution)/shard_map/pallas_call | solution.py:537
  97.1 2.9 %shard_map.93 = (bf16[256,128]{1,0:T(8,128)(2,1)}, bf16[256,128]{1,0:T(8,128)(2,1)}, bf16[448,1024]{1,0:T(8,128)(2,1)}, bf16[448,1024]{1,0:T(8,128)(2,1)}, bf16[448,1024]{1,0:T(8,128)(2,1)}) custom-call(bf16[256,128]{1,0:T(8,128)(2,1)} %get-tuple-element.15.refs_0_, bf16[256,128]{1,0:T(8,128)(2,1)} %get-tuple-element.16.refs_1_, ...), custom_call_target="tpu_custom_call" | custom-call | tf_op jit(solution)/shard_map/pallas_call | solution.py:502

commit v3 on v2

--- a/solution.py
+++ b/solution.py
@@ -466,7 +466,7 @@
     GU.a(1); GU.b(2); C.s2(); C.s3(); X.s8(); GU.b(1); GU.d(0); C.s4b(); H.a(0); GU.a(3); GU.c(2); C.s4()
     GU.b(3); GU.c(1); C.s7(); C.s5(); H.b(0); C.s6(); S.a(1); S.a(2); GU.d(2); GU.c(3); S.b(2); C.s8()
     H.a(2); S.a(3); H.c(0); S.b(3); H.d(0); S.b(1); O.part(0); GU.d(3); H.a(3); GU.d(1); H.a(1); O.c1o()
-    S.c(3); H.b(2); H.b(3); S.c(2); S.a(0); O.c1q(); S.c(1); S.d(3); G.a(3); H.b(1); H.c(2); H.c(3); H.d(2)
+    S.c(3); H.b(2); H.b(3); S.c(2); S.c(1); S.a(0); O.c1q(); S.d(3); G.a(3); H.b(1); H.c(2); H.c(3); H.d(2)
     S.d(2); G.a(2); H.d(3); O.part(3); O.x1(3); O.y1(); O.part(2); O.x1(2); G.b(3); S.b(0); O.x2(3); H.c(1)
     S.d(1); G.a(1); O.x2(2); H.d(1); O.part(1); O.y2p(); O.y2m(); G.c(3); O.x3(3); G.b(2); S.c(0); O.x1(1)
     G.d(3); I.part(3); I.x1(3); G.b(1); O.x3(2); I.y1(); O.x2(1); G.c(2); O.b1(); I.x2(3); S.d(0); G.a(0)

time: 101 us -> 101 us (level)
  no operation moved by 1% of the time
where the time goes in v3:
time: 101 us
  Pallas kernels  99.9 us (99%)
    pallas_call x1, Pallas kernels, local(): pl.pallas_call(kernel, out_shape=[sds((ct, fs), BF), sds((ct, fs), BF), s...  97 us
    pallas_call x1, Pallas kernels, publish(): pl.pallas_call(publish_kernel, out_shape=[jax.ShapeDtypeStruct(a.shape, a...  2.87 us

profile of v3, /device:TPU:1, one launch (start us, length us, event | category | flops | bytes accessed | tf_op | source)
XLA Modules:
  0.0 100.7 jit_solution(16473049170191043443)
XLA Ops:
  0.6 97.0 %shard_map.92 = (bf16[256,128]{1,0:T(8,128)(2,1)}, bf16[256,128]{1,0:T(8,128)(2,1)}, bf16[448,1024]{1,0:T(8,128)(2,1)}, bf16[448,1024]{1,0:T(8,128)(2,1)}, bf16[448,1024]{1,0:T(8,128)(2,1)}) custom-call(bf16[256,128]{1,0:T(8,128)(2,1)} %tok_hbm.1, bf16[4,112,1024]{2,1,0:T(8,128)(2,1)} %bitcast.8, bf16[4,112,1024]{2,1,0:T(8,128)(2,1)} %bitcast.9, ...), custom_call_target="tpu_custom_call" | custom-call | tf_op jit(solution)/shard_map/pallas_call | solution.py:537
  97.6 2.9 %shard_map.93 = (bf16[256,128]{1,0:T(8,128)(2,1)}, bf16[256,128]{1,0:T(8,128)(2,1)}, bf16[448,1024]{1,0:T(8,128)(2,1)}, bf16[448,1024]{1,0:T(8,128)(2,1)}, bf16[448,1024]{1,0:T(8,128)(2,1)}) custom-call(bf16[256,128]{1,0:T(8,128)(2,1)} %get-tuple-element.15.refs_0_, bf16[256,128]{1,0:T(8,128)(2,1)} %get-tuple-element.16.refs_1_, ...), custom_call_target="tpu_custom_call" | custom-call | tf_op jit(solution)/shard_map/pallas_call | solution.py:502
